TPU v7x, 128 devices: a whole 4x4x4 slice. The times are simulated.
128 devices in a mesh: dp: 8 (over x_hi, y), fsdp: 16 (over x_lo, z, core).
Axes of the slice: x: 4 (x_hi: 2, x_lo: 2; x = x_hi * 2 + x_lo), y: 4, z: 4, core: 2. Of those that a mesh axis runs over, the one named last changes fastest.
Arguments:
- queries: bfloat16 [16384, 2048], P(('dp', 'fsdp')), may hold values from -16 to 16
- doc_kv: bfloat16 [2, 8, 512, 2048], P(None, 'dp', 'fsdp'), may hold values from -12 to 12
- residual: bfloat16 [16384, 4096], P(('dp', 'fsdp')), may hold values from -25 to 25
- out_weight: bfloat16 [2048, 4096], P(None, 'fsdp'), may hold values from -0.125 to 0.125
- out_gain: float32 [4096], replicated, may hold values from 0.1 to 1.9
- head: bfloat16 [16384, 4096], P('fsdp')
- source: int32 [8], replicated, may hold values from 0 to 7, each once
- lengths: int32 [8, 8], P('dp'), may hold values from 1 to 256, 1280 in all within a row
- sampled: int32 [16384], P(('dp', 'fsdp')), may hold values from 0 to 16383
- old_logprob: float32 [16384], P(('dp', 'fsdp')), may hold values from -13 to -7
Outputs:
- log_ratio: float32 [16384], P(('dp', 'fsdp'))
- kl_term: float32 [16384], P(('dp', 'fsdp'))
Inputs may be any that keep to these rules, and one draw needn't show every extreme that they name: Each row of lengths sums to 1280. `source`: each document appears once.
All inputs are finite; a program needn't handle non-finite values.
Results may differ from a plain program's by a relative error of at most 0.0028.
Values may be sent and summed in bfloat16 or wider, within the bound.
A program may use at most 128 MiB of HBM per device.

v0:
```python
import jax
import jax.numpy as jnp
from jax import lax
from jax.sharding import PartitionSpec as P

HEADS = 8


def joined(value, axis, join):
    pieces = jax.tree.map(lambda part: lax.all_gather(part, axis), value)
    head = jax.tree.map(lambda part: part[0], pieces)
    tail = jax.tree.map(lambda part: part[1:], pieces)
    total, _ = lax.scan(lambda total, share: (join(total, share), None), head, tail)
    return total


def attend(query_rows, keys, values, heads):
    count = query_rows.shape[0]
    width = query_rows.shape[1]
    depth = width // heads
    q3 = query_rows.reshape(count, heads, depth)
    k3 = keys.reshape(keys.shape[0], heads, depth)
    v3 = values.reshape(values.shape[0], heads, depth)
    scores = jnp.einsum("thd,lhd->htl", q3, k3, preferred_element_type=jnp.float32) * float(
        depth
    ) ** (-0.5)
    largest = jnp.max(scores, axis=2, keepdims=True)
    raised = jnp.exp(scores - largest)
    weights = (raised / jnp.sum(raised, axis=2, keepdims=True)).astype(jnp.bfloat16)
    mixed = jnp.einsum("htl,lhd->thd", weights, v3, preferred_element_type=jnp.float32)
    return mixed.reshape(count, width).astype(jnp.bfloat16)


def combine_totals(first, second):
    highest = jnp.maximum(first[0], second[0])
    total = first[1] * jnp.exp(first[0] - highest) + second[1] * jnp.exp(second[0] - highest)
    return (highest, total, first[2] + second[2])


def on_device(
    queries, doc_kv, residual, out_weight, out_gain, head, source, lengths, sampled, old_logprob
):
    shard_pos = lax.axis_index("fsdp")
    row_pos = lax.axis_index("dp")
    tok_rows = queries.shape[0]
    every_doc = lax.all_gather(doc_kv, "dp", axis=1, tiled=True)
    chosen = lax.dynamic_index_in_dim(every_doc, source[row_pos], 1, keepdims=False)
    whole_doc = lax.all_gather(chosen, "fsdp", axis=1, tiled=True)
    attended = attend(queries, whole_doc[0], whole_doc[1], HEADS)
    mixed = jnp.dot(
        attended,
        lax.all_gather(out_weight, "fsdp", axis=1, tiled=True),
        preferred_element_type=jnp.float32,
    )
    summed = mixed + residual.astype(jnp.float32)
    scale = lax.rsqrt(jnp.mean(summed * summed, axis=1, keepdims=True) + 1e-06)
    hidden = (summed * scale * out_gain[None, :]).astype(jnp.bfloat16)
    group_hidden, group_ids = (
        lax.all_gather(hidden, "fsdp", axis=0, tiled=True),
        lax.all_gather(sampled, "fsdp", axis=0, tiled=True),
    )
    vocab_rows = head.shape[0]
    logits = lax.dot_general(
        group_hidden, head, (((1,), (1,)), ((), ())), preferred_element_type=jnp.float32
    )
    columns = jnp.arange(vocab_rows, dtype=jnp.int32) + shard_pos * vocab_rows
    matches = columns[None, :] == group_ids[:, None]
    picked = jnp.sum(jnp.where(matches, logits, 0.0), axis=1)
    largest = jnp.max(logits, axis=1)
    own_start = shard_pos * tok_rows
    total = jnp.sum(jnp.exp(logits - largest[:, None]), axis=1)
    highest, total, picked = joined((largest, total, picked), "fsdp", combine_totals)
    highest = lax.dynamic_slice_in_dim(highest, own_start, tok_rows, 0)
    total = lax.dynamic_slice_in_dim(total, own_start, tok_rows, 0)
    picked = lax.dynamic_slice_in_dim(picked, own_start, tok_rows, 0)
    new_logprob = picked - (highest + jnp.log(total))
    position = shard_pos % 2 * tok_rows + jnp.arange(tok_rows, dtype=jnp.int32)
    limit = lax.dynamic_index_in_dim(lengths[0], shard_pos // 2, 0, keepdims=False)
    live = position < limit
    log_ratio = jnp.where(live, new_logprob - old_logprob, jnp.float32(0.0))
    gap = jnp.clip(old_logprob - new_logprob, -3.0, 3.0)
    kl_term = jnp.where(live, jnp.exp(gap) - gap - 1.0, jnp.float32(0.0))
    return (log_ratio, kl_term)


def solution(mesh):
    return jax.shard_map(
        on_device,
        mesh=mesh,
        in_specs=(
            P(("dp", "fsdp"), None),
            P(None, "dp", "fsdp", None),
            P(("dp", "fsdp"), None),
            P(None, "fsdp"),
            P(),
            P("fsdp", None),
            P(),
            P("dp", None),
            P(("dp", "fsdp")),
            P(("dp", "fsdp")),
        ),
        out_specs=(P(("dp", "fsdp")), P(("dp", "fsdp"))),
        check_vma=False,
    )
```

profile of v0, /device:TPU:1, one launch (start us, length us, event | category | flops | bytes accessed | tf_op | source)
XLA Modules:
  0.0 398.0 jit_solution(15612936221681823901)
XLA Ops:
  7.2 1.9 copy.19
  9.2 1.2 dynamic_slice.31
  12.4 54.9 %all-gather.10.cloned.1.call-done = bf16[2,8,32,2048]{3,0,1,2:T(2,128)(2,1)} async-done(((bf16[2,1,32,2048]{3,0,1,2:T(2,128)(2,1)}), bf16[2,8,32,2048]{3,0,1,2:T(2,128)(2,1)}) %all-gather.10.cloned.1.call-update) | async-done | bytes 2097168 | tf_op jit(solution)/shard_map/all_gather | solution.py:46
  67.3 1.8 constant_dynamic-slice_fusion.3
  70.0 35.5 %all-gather.16.cloned.1.call-done = bf16[2,1,512,2048]{3,0,1,2:T(2,128)(2,1)} async-done(((bf16[2,1,32,2048]{3,0,1,2:T(2,128)(2,1)}), bf16[2,1,512,2048]{3,0,1,2:T(2,128)(2,1)}) %all-gather.16.cloned.1.call-update) | async-done | bytes 4194320 | tf_op jit(solution)/shard_map/all_gather | solution.py:48
  105.5 10.3 %fusion.19 = (bf16[1,1,512,2048]{3,0,1,2:T(2,128)(2,1)}, bf16[1,1,512,2048]{3,0,1,2:T(2,128)(2,1)}) fusion(bf16[2,1,512,2048]{3,0,1,2:T(2,128)(2,1)} %all-gather.16.cloned.1.call-done), kind=kLoop, calls=%fused_computation.34 | loop fusion | bytes 8388608 | tf_op jit(solution)/shard_map/slice | solution.py:49
  115.8 9.1 %copy.27 = bf16[1,1,512,2048]{2,3,1,0:T(8,128)(2,1)S(1)} copy(bf16[1,1,512,2048]{3,0,1,2:T(2,128)(2,1)} %get-tuple-element.66) | data formatting | bytes 4194304
  125.0 10.7 %copy.20 = bf16[1,1,512,2048]{2,3,1,0:T(8,128)(2,1)} copy(bf16[1,1,512,2048]{3,0,1,2:T(2,128)(2,1)} %get-tuple-element.67) | data formatting | bytes 4194304 | tf_op jit(solution)/shard_map/slice | solution.py:49
  136.6 1.3 copy-done.3
  138.4 1.0 copy-done.2
  139.5 4.3 %convolution_convert_fusion = bf16[8,256,128]{2,1,0:T(8,128)(2,1)} fusion(bf16[512,8,256]{0,2,1:T(8,128)(2,1)S(1)} %bitcast.48, f32[8,128]{1,0:T(8,128)S(1)} %fusion.20, f32[8,512,128]{2,1,0:T(8,128)} %copy-done.3), kind=kOutput, calls=%fused_computation.16 | convolution fusion | flops 271320576 | bytes 4722688 | tf_op jit(solution)/shard_map/htl,lhd->thd/dot_general | solution.py:30
  143.7 63.0 %all-gather.12.cloned.1.call-done = bf16[2048,4096]{1,0:T(8,128)(2,1)} async-done(((bf16[2048,256]{1,0:T(8,128)(2,1)}), bf16[2048,4096]{1,0:T(8,128)(2,1)}) %all-gather.12.cloned.1.call-update) | async-done | bytes 16777232 | tf_op jit(solution)/shard_map/all_gather | solution.py:52
  206.7 8.6 %multiply_reduce_fusion = (f32[128]{0:T(128)S(1)}, f32[128,4096]{1,0:T(8,128)S(1)}) fusion(bf16[128,4096]{1,0:T(8,128)(2,1)S(1)} %copy-done.4, bf16[128,2048]{0,1:T(8,128)(2,1)} %bitcast.52, bf16[2048,4096]{1,0:T(8,128)(2,1)} %all-gather.12.cloned.1.call-done), kind=kOutput, calls=%fused_computation.13 | convolution fusion | flops 2149580800 | bytes 20447744 | tf_op jit(solution)/shard_map/dot_general | solution.py:50
  215.3 1.3 multiply_convert_fusion
  217.3 17.7 %all-gather.4 = s32[16,1,128]{2,1,0:T(1,128)S(1)} all-gather(s32[1,1,128]{2,1,0:T(1,128)S(1)} %bitcast.55), channel_id=1, replica_groups=mesh['dp'=8,'fsdp'=16] {'fsdp'}, dimensions={0}, use_global_device_ids=true | all-gather | bytes 8704 | tf_op jit(solution)/shard_map/all_gather | solution.py:60
  235.0 73.2 %all-gather.14.cloned.1.call-done = bf16[2048,4096]{1,0:T(8,128)(2,1)} async-done(((bf16[128,4096]{1,0:T(8,128)(2,1)}), bf16[2048,4096]{1,0:T(8,128)(2,1)}) %all-gather.14.cloned.1.call-update) | async-done | bytes 16777232 | tf_op jit(solution)/shard_map/all_gather | solution.py:59
  308.2 22.8 %fusion.21 = (f32[2048]{0:T(1024)S(1)}, f32[2048,1024]{0,1:T(8,128)S(1)}) fusion(bf16[2048,4096]{1,0:T(8,128)(2,1)} %all-gather.14.cloned.1.call-done, bf16[1024,4096]{1,0:T(8,128)(2,1)} %param.17), kind=kOutput, calls=%fused_computation.36 | convolution fusion | flops 17181964288 | bytes 33562624 | tf_op jit(solution)/shard_map/dot_general | solution.py:63
  331.0 19.4 %all-gather.1 = f32[32768]{0:T(1024)S(1)} all-gather(f32[2048]{0:T(1024)S(1)} %get-tuple-element.70), channel_id=3, replica_groups=mesh['dp'=8,'fsdp'=16] {'fsdp'}, dimensions={0}, use_global_device_ids=true | all-gather | bytes 139264 | tf_op jit(solution)/shard_map/all_gather | solution.py:10
  350.5 2.5 select_reduce_fusion
  352.9 16.6 %all-gather.2 = f32[32768]{0:T(1024)S(1)} all-gather(f32[2048]{0:T(1024)S(1)} %get-tuple-element.45), channel_id=4, replica_groups=mesh['dp'=8,'fsdp'=16] {'fsdp'}, dimensions={0}, use_global_device_ids=true | all-gather | bytes 139264 | tf_op jit(solution)/shard_map/all_gather | solution.py:10
  369.6 17.9 %all-gather.3 = f32[32768]{0:T(1024)S(1)} all-gather(f32[2048]{0:T(1024)S(1)} %get-tuple-element.44), channel_id=5, replica_groups=mesh['dp'=8,'fsdp'=16] {'fsdp'}, dimensions={0}, use_global_device_ids=true | all-gather | bytes 139264 | tf_op jit(solution)/shard_map/all_gather | solution.py:10
  387.6 1.5 while.14
  389.1 1.2 compare_select_fusion
  390.4 1.1 compare_select_fusion.1
  (98 shorter events, 3.9 us)
Async XLA Ops:
  7.2 209.5 %copy-start = (s32[1,8]{1,0:T(1,128)S(1)}, s32[1,8]{1,0:T(1,128)}, u32[]{:S(2)}) copy-start(s32[1,8]{1,0:T(1,128)} %param.19) | copy-start | bytes 100
  7.2 60.2 %all-gather.10.cloned.1.call-start = ((), (), s32[]{:S(2)}) async-start(), calls=%async_computation | async-start | bytes 2359296 | tf_op jit(solution)/shard_map/all_gather | solution.py:46
  9.2 96.4 %all-gather.16.cloned.1.call-start = ((), (), s32[]{:S(2)}) async-start(), calls=%async_computation.3 | async-start | bytes 4456448 | tf_op jit(solution)/shard_map/all_gather | solution.py:48
  69.2 137.5 %all-gather.12.cloned.1.call-start = ((), (), s32[]{:S(2)}) async-start(), calls=%async_computation.1 | async-start | bytes 17825792 | tf_op jit(solution)/shard_map/all_gather | solution.py:52
  69.9 238.3 %all-gather.14.cloned.1.call-start = ((), (), s32[]{:S(2)}) async-start(), calls=%async_computation.2 | async-start | bytes 17825792 | tf_op jit(solution)/shard_map/all_gather | solution.py:59
  125.0 10.7 %copy-start.5 = (bf16[128,2048]{1,0:T(8,128)(2,1)S(1)}, bf16[128,2048]{1,0:T(8,128)(2,1)}, u32[]{:S(2)}) copy-start(bf16[128,2048]{1,0:T(8,128)(2,1)} %param.12) | copy-start | bytes 1572868
  136.6 1.3 copy-start.3
  137.9 1.6 copy-start.2
  139.5 67.2 %copy-start.4 = (bf16[128,4096]{1,0:T(8,128)(2,1)S(1)}, bf16[128,4096]{1,0:T(8,128)(2,1)}, u32[]{:S(2)}) copy-start(bf16[128,4096]{1,0:T(8,128)(2,1)} %param.14) | copy-start | bytes 3145732
  206.7 8.6 %copy-start.6 = (f32[4096]{0:T(1024)S(1)}, f32[4096]{0:T(1024)}, u32[]{:S(2)}) copy-start(f32[4096]{0:T(1024)} %param.16) | copy-start | bytes 49156
  215.3 2.0 copy-start.8
  350.5 41.1 %copy-start.1 = (s32[1,8]{1,0:T(1,128)S(1)}, s32[1,8]{1,0:T(1,128)}, u32[]{:S(2)}) copy-start(s32[1,8]{1,0:T(1,128)} %param.19) | copy-start | bytes 100
  352.9 36.2 %copy-start.7 = (f32[128]{0:T(128)S(1)}, f32[128]{0:T(128)}, u32[]{:S(2)}) copy-start(f32[128]{0:T(128)} %param.21) | copy-start | bytes 1540
Sparse Core Ops, SparseCore 0:
  10.2 57.1 all-gather.9
  69.3 36.1 all-gather.15
  107.2 99.4 all-gather.11
  216.7 91.4 all-gather.13
where the time goes:
time: 399 us; the launch traced here: 398 us
  waiting for transfers between devices  227 us (57%)
  blocking collectives  71.7 us (18%)
  local copies, waits for them, and re-layouts  38.8 us (10%)
  matrix products  36.5 us (9%)
  between operations  15.9 us (4%)
  other arithmetic  6.93 us (2%)
    all_gather x1, waiting for transfers between devices, on_device(): lax.all_gather(hidden, 'fsdp', axis=0, tiled=True)  73.2 us
    all_gather x1, waiting for transfers between devices, on_device(): lax.all_gather(out_weight, 'fsdp', axis=1, tiled=True)  63 us
    all_gather x1, waiting for transfers between devices, on_device(): every_doc = lax.all_gather(doc_kv, 'dp', axis=1, tiled=True)  54.9 us
    all_gather x3, blocking collectives, joined(): pieces = jax.tree.map(lambda part: lax.all_gather(part, axis), value)  54 us
    all_gather x1, waiting for transfers between devices, on_device(): whole_doc = lax.all_gather(chosen, 'fsdp', axis=1, tiled=True)  35.5 us
    dot_general x1, matrix products, on_device(): lax.dot_general(group_hidden, head, (((1,), (1,)), ((), ())), preferred_e...  22.8 us
    slice x2, local copies, waits for them, and re-layouts, on_device(): attended = attend(queries, whole_doc[0], whole_doc[1], HEADS)  21 us
    all_gather x1, blocking collectives, on_device(): lax.all_gather(sampled, 'fsdp', axis=0, tiled=True)  17.7 us
  transfers between devices with their start and end apart: 4, of which 4 were waited for; matrix products, arithmetic and copies ran while one was open for 9% of the time, Pallas kernels for 0%

commit v1 on v0

--- a/solution.py
+++ b/solution.py
@@ -49,7 +49,9 @@
     attended = attend(queries, whole_doc[0], whole_doc[1], HEADS)
     mixed = jnp.dot(
         attended,
-        lax.all_gather(out_weight, "fsdp", axis=1, tiled=True),
+        jnp.concatenate(
+            lax.all_to_all(jnp.stack([out_weight] * lax.axis_size("fsdp")), "fsdp", 0, 0), axis=1
+        ),
         preferred_element_type=jnp.float32,
     )
     summed = mixed + residual.astype(jnp.float32)

time: 399 us -> 495 us (1.24)
  waiting for transfers between devices: 227 us -> 302 us
  starting transfers between devices: 0.16 us -> 8.01 us
  local copies, waits for them, and re-layouts: 38.8 us -> 44 us
  blocking collectives: 71.7 us -> 76.8 us
    all_gather x1, waiting for transfers between devices: 35.5 us -> 123 us  [on_device(): whole_doc = lax.all_gather(chosen, 'fsdp', axis=1, tiled=True)]
    all_gather x1 -> x0, waiting for transfers between devices: 63 us -> none  [on_device(): lax.all_gather(out_weight, 'fsdp', axis=1, tiled=True)]
    all_to_all x0 -> x1, waiting for transfers between devices: none -> 36.6 us  [on_device(): lax.all_to_all(jnp.stack([out_weight] * lax.axis_size('fsdp')), 'fsdp', 0...]
    all_gather x1, waiting for transfers between devices: 54.9 us -> 69.1 us  [on_device(): every_doc = lax.all_gather(doc_kv, 'dp', axis=1, tiled=True)]
    all_to_all x0 -> x1, starting transfers between devices: none -> 7.89 us  [on_device(): lax.all_to_all(jnp.stack([out_weight] * lax.axis_size('fsdp')), 'fsdp', 0...]
    another operation x0 -> x1, local copies, waits for them, and re-layouts: none -> 5.99 us  [on_device(): jnp.stack([out_weight] * lax.axis_size('fsdp'))]
    all_gather x1, blocking collectives: 17.7 us -> 22.8 us  [on_device(): lax.all_gather(sampled, 'fsdp', axis=0, tiled=True)]
    unnamed x20 -> x25, local copies, waits for them, and re-layouts: 13.4 us -> 13.9 us
  transfers between devices with their start and end apart: 4 -> 4, of which waited for: 4 -> 4; matrix products, arithmetic and copies ran while one was open for 9% -> 8% of each run, Pallas kernels for 0% -> 0%
where the time goes in v1:
time: 495 us; the launch traced here: 494 us
  waiting for transfers between devices  302 us (61%)
  blocking collectives  76.8 us (16%)
  local copies, waits for them, and re-layouts  44 us (9%)
  matrix products  39.6 us (8%)
  between operations  15.9 us (3%)
  starting transfers between devices  8.01 us (2%)
  other arithmetic  6.93 us (1%)
    all_gather x1, waiting for transfers between devices, on_device(): whole_doc = lax.all_gather(chosen, 'fsdp', axis=1, tiled=True)  123 us
    all_gather x1, waiting for transfers between devices, on_device(): lax.all_gather(hidden, 'fsdp', axis=0, tiled=True)  73.4 us
    all_gather x1, waiting for transfers between devices, on_device(): every_doc = lax.all_gather(doc_kv, 'dp', axis=1, tiled=True)  69.1 us
    all_gather x3, blocking collectives, joined(): pieces = jax.tree.map(lambda part: lax.all_gather(part, axis), value)  54 us
    all_to_all x1, waiting for transfers between devices, on_device(): lax.all_to_all(jnp.stack([out_weight] * lax.axis_size('fsdp')), 'fsdp', 0...  36.6 us
    dot_general x1, matrix products, on_device(): lax.dot_general(group_hidden, head, (((1,), (1,)), ((), ())), preferred_e...  22.8 us
    all_gather x1, blocking collectives, on_device(): lax.all_gather(sampled, 'fsdp', axis=0, tiled=True)  22.8 us
    slice x2, local copies, waits for them, and re-layouts, on_device(): attended = attend(queries, whole_doc[0], whole_doc[1], HEADS)  20.5 us
  transfers between devices with their start and end apart: 4, of which 4 were waited for; matrix products, arithmetic and copies ran while one was open for 8% of the time, Pallas kernels for 0%

profile of v1, /device:TPU:1, one launch (start us, length us, event | category | flops | bytes accessed | tf_op | source)
XLA Modules:
  0.0 494.1 jit_solution(13651926902195945142)
XLA Ops:
  7.2 1.5 copy.26
  8.7 6.0 %stack.2 = bf16[16,2048,256]{1,2,0:T(8,128)(2,1)} broadcast(bf16[2048,256]{0,1:T(8,128)(2,1)S(1)} %copy.26), dimensions={1,2} | broadcast | bytes 17825792 | tf_op jit(solution)/shard_map/stack | solution.py:53
  14.7 7.9 %all-to-all-start = ((bf16[16,2048,256]{1,2,0:T(8,128)(2,1)}), bf16[16,2048,256]{1,2,0:T(8,128)(2,1)}, u32[]{:S(2)}, u32[]{:S(2)}) async-start(bf16[16,2048,256]{1,2,0:T(8,128)(2,1)} %stack.2), calls=%async_computation | async-start | bytes 33554432 | tf_op jit(solution)/shard_map/all_to_all | solution.py:53
  26.2 69.1 %all-gather.9.cloned.1.call-done = bf16[2,8,32,2048]{3,0,1,2:T(2,128)(2,1)} async-done(((bf16[2,1,32,2048]{3,0,1,2:T(2,128)(2,1)}), bf16[2,8,32,2048]{3,0,1,2:T(2,128)(2,1)}) %all-gather.9.cloned.1.call-update) | async-done | bytes 2097168 | tf_op jit(solution)/shard_map/all_gather | solution.py:46
  95.3 1.8 constant_dynamic-slice_fusion.3
  97.2 123.0 %all-gather.13.cloned.1.call-done = bf16[2,1,512,2048]{3,0,1,2:T(2,128)(2,1)} async-done(((bf16[2,1,32,2048]{3,0,1,2:T(2,128)(2,1)}), bf16[2,1,512,2048]{3,0,1,2:T(2,128)(2,1)}) %all-gather.13.cloned.1.call-update) | async-done | bytes 4194320 | tf_op jit(solution)/shard_map/all_gather | solution.py:48
  220.3 10.0 %fusion.19 = (bf16[1,1,512,2048]{3,0,1,2:T(2,128)(2,1)}, bf16[1,1,512,2048]{3,0,1,2:T(2,128)(2,1)}) fusion(bf16[2,1,512,2048]{3,0,1,2:T(2,128)(2,1)} %all-gather.13.cloned.1.call-done), kind=kLoop, calls=%fused_computation.34 | loop fusion | bytes 8388608 | tf_op jit(solution)/shard_map/slice | solution.py:49
  230.2 9.0 %copy.29 = bf16[1,1,512,2048]{2,3,1,0:T(8,128)(2,1)S(1)} copy(bf16[1,1,512,2048]{3,0,1,2:T(2,128)(2,1)} %get-tuple-element.66) | data formatting | bytes 4194304
  239.2 10.5 %copy.21 = bf16[1,1,512,2048]{2,3,1,0:T(8,128)(2,1)} copy(bf16[1,1,512,2048]{3,0,1,2:T(2,128)(2,1)} %get-tuple-element.67) | data formatting | bytes 4194304 | tf_op jit(solution)/shard_map/slice | solution.py:49
  250.6 1.4 copy-done.3
  253.6 4.3 convolution_convert_fusion
  257.9 36.6 %all-to-all-done = bf16[16,2048,256]{1,2,0:T(8,128)(2,1)} async-done(((bf16[16,2048,256]{1,2,0:T(8,128)(2,1)}), bf16[16,2048,256]{1,2,0:T(8,128)(2,1)}, u32[]{:S(2)}, u32[]{:S(2)}) %all-to-all-start) | async-done | bytes 16777248 | tf_op jit(solution)/shard_map/all_to_all | solution.py:53
  294.5 11.7 %multiply_reduce_fusion = (f32[128]{0:T(128)S(1)}, f32[128,4096]{1,0:T(8,128)S(1)}) fusion(bf16[128,4096]{1,0:T(8,128)(2,1)S(1)} %copy-done.4, bf16[128,2048]{0,1:T(8,128)(2,1)} %bitcast.56, bf16[2048,4096]{0,1:T(8,128)(2,1)} %bitcast.11), kind=kOutput, calls=%fused_computation.13 | convolution fusion | flops 2149580800 | bytes 20447744 | tf_op jit(solution)/shard_map/dot_general | solution.py:50
  306.1 1.3 multiply_convert_fusion
  308.1 22.8 %all-gather.4 = s32[16,1,128]{2,1,0:T(1,128)S(1)} all-gather(s32[1,1,128]{2,1,0:T(1,128)S(1)} %bitcast.58), channel_id=1, replica_groups=mesh['dp'=8,'fsdp'=16] {'fsdp'}, dimensions={0}, use_global_device_ids=true | all-gather | bytes 8704 | tf_op jit(solution)/shard_map/all_gather | solution.py:62
  330.8 73.4 %all-gather.11.cloned.1.call-done = bf16[2048,4096]{1,0:T(8,128)(2,1)} async-done(((bf16[128,4096]{1,0:T(8,128)(2,1)}), bf16[2048,4096]{1,0:T(8,128)(2,1)}) %all-gather.11.cloned.1.call-update) | async-done | bytes 16777232 | tf_op jit(solution)/shard_map/all_gather | solution.py:61
  404.3 22.8 %fusion.21 = (f32[2048]{0:T(1024)S(1)}, f32[2048,1024]{0,1:T(8,128)S(1)}) fusion(bf16[2048,4096]{1,0:T(8,128)(2,1)} %all-gather.11.cloned.1.call-done, bf16[1024,4096]{1,0:T(8,128)(2,1)} %param.17), kind=kOutput, calls=%fused_computation.36 | convolution fusion | flops 17181964288 | bytes 33562624 | tf_op jit(solution)/shard_map/dot_general | solution.py:65
  427.1 19.4 %all-gather.1 = f32[32768]{0:T(1024)S(1)} all-gather(f32[2048]{0:T(1024)S(1)} %get-tuple-element.70), channel_id=3, replica_groups=mesh['dp'=8,'fsdp'=16] {'fsdp'}, dimensions={0}, use_global_device_ids=true | all-gather | bytes 139264 | tf_op jit(solution)/shard_map/all_gather | solution.py:10
  446.5 2.5 select_reduce_fusion
  449.0 16.6 %all-gather.2 = f32[32768]{0:T(1024)S(1)} all-gather(f32[2048]{0:T(1024)S(1)} %get-tuple-element.45), channel_id=4, replica_groups=mesh['dp'=8,'fsdp'=16] {'fsdp'}, dimensions={0}, use_global_device_ids=true | all-gather | bytes 139264 | tf_op jit(solution)/shard_map/all_gather | solution.py:10
  465.6 17.9 %all-gather.3 = f32[32768]{0:T(1024)S(1)} all-gather(f32[2048]{0:T(1024)S(1)} %get-tuple-element.44), channel_id=5, replica_groups=mesh['dp'=8,'fsdp'=16] {'fsdp'}, dimensions={0}, use_global_device_ids=true | all-gather | bytes 139264 | tf_op jit(solution)/shard_map/all_gather | solution.py:10
  483.7 1.5 while.14
  485.2 1.2 compare_select_fusion
  486.5 1.1 compare_select_fusion.1
  (103 shorter events, 5.7 us)
Async XLA Ops:
  7.2 300.3 %copy-start = (s32[1,8]{1,0:T(1,128)S(1)}, s32[1,8]{1,0:T(1,128)}, u32[]{:S(2)}) copy-start(s32[1,8]{1,0:T(1,128)} %param.19) | copy-start | bytes 100
  14.7 7.9 %copy-start.6 = (bf16[2,1,32,2048]{3,2,1,0:T(8,128)(2,1)S(1)}, bf16[2,1,32,2048]{3,2,1,0:T(8,128)(2,1)}, u32[]{:S(2)}) copy-start(bf16[2,1,32,2048]{3,2,1,0:T(8,128)(2,1)} %param.13) | copy-start | bytes 786436
  14.7 9.0 %copy-start.10 = (s32[8]{0:T(128)S(1)}, s32[8]{0:T(128)}, u32[]{:S(2)}) copy-start(s32[8]{0:T(128)} %param.18) | copy-start | bytes 100
  14.7 279.8 %all-to-all-start = ((bf16[16,2048,256]{1,2,0:T(8,128)(2,1)}), bf16[16,2048,256]{1,2,0:T(8,128)(2,1)}, u32[]{:S(2)}, u32[]{:S(2)}) async-start(bf16[16,2048,256]{1,2,0:T(8,128)(2,1)} %stack.2), calls=%async_computation | async-start | bytes 33554432 | tf_op jit(solution)/shard_map/all_to_all | solution.py:53
  22.6 72.8 %all-gather.9.cloned.1.call-start = ((), (), s32[]{:S(2)}) async-start(), calls=%async_computation.1 | async-start | bytes 2359296 | tf_op jit(solution)/shard_map/all_gather | solution.py:46
  23.6 196.7 %all-gather.13.cloned.1.call-start = ((), (), s32[]{:S(2)}) async-start(), calls=%async_computation.3 | async-start | bytes 4456448 | tf_op jit(solution)/shard_map/all_gather | solution.py:48
  97.2 307.1 %all-gather.11.cloned.1.call-start = ((), (), s32[]{:S(2)}) async-start(), calls=%async_computation.2 | async-start | bytes 17825792 | tf_op jit(solution)/shard_map/all_gather | solution.py:61
  239.2 10.5 %copy-start.5 = (bf16[128,2048]{1,0:T(8,128)(2,1)S(1)}, bf16[128,2048]{1,0:T(8,128)(2,1)}, u32[]{:S(2)}) copy-start(bf16[128,2048]{1,0:T(8,128)(2,1)} %param.12) | copy-start | bytes 1572868
  250.6 1.4 copy-start.3
  252.0 1.6 copy-start.2
  253.6 40.9 %copy-start.4 = (bf16[128,4096]{1,0:T(8,128)(2,1)S(1)}, bf16[128,4096]{1,0:T(8,128)(2,1)}, u32[]{:S(2)}) copy-start(bf16[128,4096]{1,0:T(8,128)(2,1)} %param.14) | copy-start | bytes 3145732
  294.5 11.7 %copy-start.7 = (f32[4096]{0:T(1024)S(1)}, f32[4096]{0:T(1024)}, u32[]{:S(2)}) copy-start(f32[4096]{0:T(1024)} %param.16) | copy-start | bytes 49156
  306.1 1.9 copy-start.9
  446.5 41.1 %copy-start.1 = (s32[1,8]{1,0:T(1,128)S(1)}, s32[1,8]{1,0:T(1,128)}, u32[]{:S(2)}) copy-start(s32[1,8]{1,0:T(1,128)} %param.19) | copy-start | bytes 100
  449.0 36.2 %copy-start.8 = (f32[128]{0:T(128)S(1)}, f32[128]{0:T(128)}, u32[]{:S(2)}) copy-start(f32[128]{0:T(128)} %param.21) | copy-start | bytes 1540
Sparse Core Ops, SparseCore 0:
  25.6 69.7 all-gather.8
  97.3 122.9 all-gather.12
  307.5 96.6 all-gather.10
